TPU v7x, 1024 devices: a whole 8x8x8 slice. The times are simulated.
1024 devices in a mesh: pair: 64 (over y, z_lo, core), virt: 16 (over z_hi, x).
Axes of the slice: x: 8, y: 8, z: 8 (z_hi: 2, z_lo: 4; z = z_hi * 4 + z_lo), core: 2. Of those that a mesh axis runs over, the one named last changes fastest.
Arguments:
- amplitudes: bfloat16 [384, 16, 128, 2048], P('pair', None, None, 'virt'), may hold values from -6 to 6
- integrals: bfloat16 [128, 2048, 128], P('pair', 'virt'), may hold values from -0.03125 to 0.03125
- tile_blocks: int32 [384, 2], P('pair'), may hold values from 0 to 31, as said below
- occ_irrep: int32 [128], replicated, may hold values from 0 to 7
- slab_irrep: int32 [128], replicated, may hold values from 0 to 7
- virt_irrep: int32 [2048], P('virt'), may hold values from 0 to 7
- ab_irrep: int32 [128], replicated, may hold values from 0 to 7
- occ_energy: float32 [128], replicated, may hold values from -2 to -0.5
- ab_energy: float32 [128], replicated, may hold values from 0.5 to 4
Outputs:
- update: float32 [384, 16, 128], P('pair')
Inputs may be any that keep to these rules, and one draw needn't show every extreme that they name: `tile_blocks`: each row is two different blocks; with H = 32, the tile at position t * 6 + s holds the blocks of the tile at ((t + H) % (2 * H)) * 6 + s in reverse order.
All inputs are finite; a program needn't handle non-finite values.
Results may differ from a plain program's by a relative error of at most 0.0003.
Values may be sent and summed in bfloat16 or wider, within the bound.
A program may use at most 32 MiB of HBM per device.

v0:
```python
import jax
import jax.numpy as jnp
from jax import lax
from jax.sharding import PartitionSpec as P

OB = 4


def from_behind(array, axis, by):
    peers = lax.axis_size(axis)
    return lax.ppermute(array, axis, [(i, (i + by) % peers) for i in range(peers)])


def mirrored(ladder):
    count = lax.axis_size("pair")
    return from_behind(ladder, "pair", count // 2)


def finish(ladder, pair_irrep, pair_energy, energy_cols, irrep_cols, tiles):
    width = ladder.shape[1]
    other = mirrored(ladder)
    other = jnp.swapaxes(other.reshape(tiles, OB, OB, width), 1, 2).reshape(tiles, OB * OB, width)
    combined = 0.5 * (ladder.reshape(tiles, OB * OB, width) - other)
    denom = pair_energy[:, :, None] - energy_cols[None, None, :]
    keep = jnp.bitwise_xor(pair_irrep[:, :, None], irrep_cols[None, None, :]) == 0
    return jnp.where(keep, combined / denom, jnp.zeros((), combined.dtype))


def on_device(
    amplitudes,
    integrals,
    tile_blocks,
    occ_irrep,
    slab_irrep,
    virt_irrep,
    ab_irrep,
    occ_energy,
    ab_energy,
):
    tiles = amplitudes.shape[0]
    local = jnp.arange(OB * OB, dtype=jnp.int32)
    occ_i = tile_blocks[:, 0:1] * OB + (local // OB)[None, :]
    occ_j = tile_blocks[:, 1:2] * OB + (local % OB)[None, :]
    pair_irrep = jnp.bitwise_xor(occ_irrep[occ_i], occ_irrep[occ_j])
    pair_energy = occ_energy[occ_i] + occ_energy[occ_j]
    cd_irrep = jnp.bitwise_xor(slab_irrep[:, None], virt_irrep[None, :])
    keep = jnp.bitwise_xor(pair_irrep[:, :, None, None], cd_irrep[None, None]) == 0
    masked = jnp.where(keep, amplitudes, jnp.zeros((), amplitudes.dtype))
    rows = masked.reshape(tiles * OB * OB, amplitudes.shape[2], amplitudes.shape[3])
    partial_sums = jnp.einsum(
        "rcd,cdp->rp",
        rows,
        lax.all_gather(integrals, "pair", axis=0, tiled=True),
        preferred_element_type=jnp.float32,
    )
    ladder = lax.psum(partial_sums, "virt")
    return finish(ladder, pair_irrep, pair_energy, ab_energy, ab_irrep, tiles)


def solution(mesh):
    return jax.shard_map(
        on_device,
        mesh=mesh,
        in_specs=(
            P("pair", None, None, "virt"),
            P("pair", "virt", None),
            P("pair", None),
            P(),
            P(),
            P("virt"),
            P(),
            P(),
            P(),
        ),
        out_specs=P("pair", None, None),
        check_vma=False,
    )
```

profile of v0, /device:TPU:16, one launch (start us, length us, event | category | flops | bytes accessed | tf_op | source)
XLA Modules:
  0.0 264.4 jit_solution(10018833706374811018)
XLA Ops:
  6.5 0.0 copy-start
  6.5 0.7 all-gather.2.cloned.1.call-update
  7.3 0.8 multiply_bitcast_fusion
  8.0 0.1 compare_select_fusion
  8.1 0.1 reshape.194
  8.2 0.1 reshape.202
  8.3 1.2 gather_fusion
  9.5 0.0 copy-start.2
  9.5 0.0 copy-start.3
  9.6 1.2 gather_fusion.1
  10.8 0.1 reshape.228
  10.9 0.1 broadcast_xor_fusion
  11.0 3.0 %fusion = bf16[6,16,128,128]{3,2,1,0:T(8,128)(2,1)S(1)} fusion(bf16[6,16,128,128]{3,2,1,0:T(8,128)(2,1)} %param.9, s32[128,128]{1,0:T(8,128)S(1)} %broadcast_xor_fusion, s32[6,16]{1,0:T(8,128)S(1)} %reshape.228), kind=kLoop, calls=%fused_computation.5 | loop fusion | flops 4718592 | bytes 6357376 | tf_op jit(solution)/shard_map/jit(_where)/select_n | solution.py:48
  14.0 130.1 %all-gather.2.cloned.1.call-done = bf16[128,128,128]{2,1,0:T(8,128)(2,1)} async-done(((bf16[2,128,128]{2,1,0:T(8,128)(2,1)}), bf16[128,128,128]{2,1,0:T(8,128)(2,1)}) %all-gather.2.cloned.1.call-update) | async-done | bytes 4194320 | tf_op jit(solution)/shard_map/all_gather | solution.py:53
  144.1 4.4 %fusion.3 = f32[96,128]{1,0:T(8,128)S(1)} fusion(bf16[128,128,128]{2,1,0:T(8,128)(2,1)} %all-gather.2.cloned.1.call-done, bf16[96,128,128]{2,1,0:T(8,128)(2,1)S(1)} %bitcast.17), kind=kOutput, calls=%fused_computation.8 | convolution fusion | flops 402653184 | bytes 7389184 | tf_op jit(solution)/shard_map/rcd,cdp->rp/dot_general | solution.py:50
  148.5 98.4 %psum.7 = f32[96,128]{1,0:T(8,128)S(1)} all-reduce(f32[96,128]{1,0:T(8,128)S(1)} %fusion.3), channel_id=1, replica_groups=mesh['pair'=64,'virt'=16] {'virt'}, use_global_device_ids=true, to_apply=%region_0.1 | all-reduce | flops 12288 | bytes 98304 | tf_op jit(solution)/shard_map/psum | solution.py:56
  246.9 4.3 %collective-permute-start = (f32[96,128]{1,0:T(8,128)S(1)}, f32[96,128]{1,0:T(8,128)S(1)}, u32[]{:S(2)}, u32[]{:S(2)}) collective-permute-start(f32[96,128]{1,0:T(8,128)S(1)} %psum.7), channel_id=1, source_target_pairs={{0,512},{16,528},{32,544},{48,560},{64,576},{80,592},{96,608},{112... | collective-permute-start | bytes 147464 | tf_op jit(solution)/shard_map/ppermute | solution.py:11
  251.3 1.2 gather_fusion.2
  252.5 0.0 copy-start.4
  252.5 0.0 copy-start.5
  252.5 1.2 gather_fusion.3
  253.8 0.1 reshape.229
  253.9 2.9 %collective-permute-done = f32[96,128]{1,0:T(8,128)S(1)} collective-permute-done((f32[96,128]{1,0:T(8,128)S(1)}, f32[96,128]{1,0:T(8,128)S(1)}, u32[]{:S(2)}, u32[]{:S(2)}) %collective-permute-start) | collective-permute-done | bytes 49184 | tf_op jit(solution)/shard_map/ppermute | solution.py:11
  256.8 0.7 divide_select_fusion
  (15 shorter events, 0.1 us)
Async XLA Ops:
  6.5 1.8 copy-start
  6.5 137.5 %all-gather.2.cloned.1.call-start = ((), (), s32[]{:S(2)}) async-start(), calls=%async_computation | async-start | bytes 4259840 | tf_op jit(solution)/shard_map/all_gather | solution.py:53
  9.5 1.4 copy-start.2
  9.5 1.4 copy-start.3
  144.1 107.2 %copy-start.1 = (f32[128]{0:T(128)S(1)}, f32[128]{0:T(128)}, u32[]{:S(2)}) copy-start(f32[128]{0:T(128)} %param.16) | copy-start | bytes 1540
  246.9 9.9 %collective-permute-start = (f32[96,128]{1,0:T(8,128)S(1)}, f32[96,128]{1,0:T(8,128)S(1)}, u32[]{:S(2)}, u32[]{:S(2)}) collective-permute-start(f32[96,128]{1,0:T(8,128)S(1)} %psum.7), channel_id=1, source_target_pairs={{0,512},{16,528},{32,544},{48,560},{64,576},{80,592},{96,608},{112... | collective-permute-start | bytes 147464 | tf_op jit(solution)/shard_map/ppermute | solution.py:11
  252.5 4.3 %copy-start.4 = (f32[128]{0:T(128)S(1)}, f32[128]{0:T(128)}, u32[]{:S(2)}) copy-start(f32[128]{0:T(128)} %param.17) | copy-start | bytes 1540
  252.5 4.3 %copy-start.5 = (s32[128]{0:T(128)S(1)}, s32[128]{0:T(128)}, u32[]{:S(2)}) copy-start(s32[128]{0:T(128)} %param.15) | copy-start | bytes 1540
Sparse Core Ops, SparseCore 0:
  10.1 133.9 all-gather.1
where the time goes:
time: 265 us; the launch traced here: 264 us
  waiting for transfers between devices  134 us (51%)
  blocking collectives  98.4 us (37%)
  between operations  13.6 us (5%)
  local copies, waits for them, and re-layouts  5.26 us (2%)
  other arithmetic  4.63 us (2%)
  matrix products  4.44 us (2%)
  starting transfers between devices  4.34 us (2%)
    all_gather x1, waiting for transfers between devices, on_device(): lax.all_gather(integrals, 'pair', axis=0, tiled=True)  130 us
    psum x1, blocking collectives, on_device(): ladder = lax.psum(partial_sums, 'virt')  98.4 us
  transfers between devices with their start and end apart: 2, of which 2 were waited for; matrix products, arithmetic and copies ran while one was open for 3% of the time, Pallas kernels for 0%

commit v1 on v0

v1 whole, which is shorter than its diff:
```python
import functools

import jax
import jax.numpy as jnp
from jax import lax
from jax.experimental import pallas as pl
from jax.experimental.pallas import tpu as pltpu
from jax.sharding import PartitionSpec as P

OB = 4
TILES = 6
ROWS = TILES * OB * OB
LANES = 128
WIDTH = 32
HALF = WIDTH // 2
NY, NZ, NCORE, NX, NH = 8, 4, 2, 8, 2
PITCH = 136
MESH = pl.DeviceIdType.MESH
NT = (((1,), (1,)), ((), ()))
TN = (((0,), (0,)), ((), ()))


def place():
    pair, virt = lax.axis_index("pair"), lax.axis_index("virt")
    return pair // (NZ * NCORE), (pair // NCORE) % NZ, pair % NCORE, virt // NX, virt % NX


def kernel(
    tile_blocks, occ_irrep, slab_scalar, occ_energy, chunk, amps, ints, virt, slab, ab, ab_energy,
    out, top,
    held, spread, rows, lo, hi, factor, over_x, over_m, result, sem_in, send, recv,
):
    y, z, core, half, x = place()
    mirror = y // (NY // 2)

    def at(dy=0, dz=0, dc=0, dh=0, dx=0):
        pair = ((y + dy) % NY) * (NZ * NCORE) + ((z + dz) % NZ) * NCORE + (core + dc) % NCORE
        return pair, ((half + dh) % NH) * NX + (x + dx) % NX

    peers = [at(dy=k) for k in range(1, NY)] + [at(dz=k) for k in range(1, NZ)] + [at(dc=1)]
    peers += [at(dx=k) for k in range(1, NX)] + [at(dh=1), at(dy=NY // 2, dh=1)]
    barrier = pltpu.get_barrier_semaphore()
    for peer in peers:
        pl.semaphore_signal(barrier, inc=1, device_id=peer, device_id_type=MESH)

    load = pltpu.make_async_copy(amps, held, sem_in)
    load.start()

    def remote(src, dst, number, peer):
        return pltpu.make_async_remote_copy(
            src_ref=src, dst_ref=dst, send_sem=send.at[number], recv_sem=recv.at[number],
            device_id=peer, device_id_type=MESH,
        )

    ab_row = ab[...]
    ab_rows = jnp.broadcast_to(ab_row, (LANES, LANES))
    ab_cols = jnp.transpose(ab_rows)
    before = lax.broadcasted_iota(jnp.int32, (LANES, LANES), 0) < lax.broadcasted_iota(jnp.int32, (LANES, LANES), 1)
    same = jnp.where((ab_rows == ab_cols) & before, 1.0, 0.0)
    rank = jnp.sum(same, axis=0, keepdims=True).astype(jnp.int32)
    top[...] = jnp.broadcast_to(jnp.max(rank, axis=1, keepdims=True), top.shape)
    slot = lax.broadcasted_iota(jnp.int32, (WIDTH, LANES), 0) + chunk[0] * WIDTH
    pick = jnp.where(slot == jnp.broadcast_to(rank, (WIDTH, LANES)), 1.0, 0.0)
    pick_narrow = pick.astype(jnp.bfloat16)
    virt_rows = jnp.broadcast_to(virt[...], (LANES, LANES))
    virt_cols = jnp.transpose(virt_rows)
    labels = jnp.bitwise_xor(virt_cols, ab_rows)
    own = (y * NZ + z) * NCORE + core
    for c in range(2):
        kept = jnp.where(labels == slab_scalar[own * 2 + c], ints[c].astype(jnp.float32), 0.0).astype(jnp.bfloat16)
        packed = lax.dot_general(pick_narrow, kept, NT, preferred_element_type=jnp.float32).astype(jnp.bfloat16)
        lo[core, y, z, :, c * LANES:(c + 1) * LANES] = packed[:HALF]
        hi[core, z, y, :, c * LANES:(c + 1) * LANES] = packed[HALF:]

    pl.semaphore_wait(barrier, len(peers))

    sends = []
    n = 0
    first = []
    for k in range(1, NZ):
        copy = remote(lo.at[core, y, z], lo.at[core, y, z], n, at(dz=k))
        copy.start()
        sends.append(copy)
        first.append(remote(lo.at[core, y, z], lo.at[core, y, (z - k + NZ) % NZ], n, at(dz=k)))
        n += 1
    for k in range(1, NY):
        copy = remote(hi.at[core, z, y], hi.at[core, z, y], n, at(dy=k))
        copy.start()
        sends.append(copy)
        first.append(remote(hi.at[core, z, y], hi.at[core, z, (y - k + NY) % NY], n, at(dy=k)))
        n += 1

    load.wait()
    cd = jnp.bitwise_xor(jnp.transpose(jnp.broadcast_to(slab[...], (LANES, LANES))), virt_rows)
    sign = (1 - 2 * mirror).astype(jnp.float32)

    def mask_tile(k, carry):
        for q in range(OB * OB):
            i, j = q // OB, q % OB
            source = k * (OB * OB) + q + mirror * (j * OB + i - q)
            a = tile_blocks[k, 0] * OB + (i + mirror * (j - i))
            b = tile_blocks[k, 1] * OB + (j + mirror * (i - j))
            irrep = jnp.bitwise_xor(occ_irrep[a], occ_irrep[b])
            energy = occ_energy[a] + occ_energy[b]
            row = k * (OB * OB) + q
            spread[pl.ds(pl.multiple_of(row * PITCH, 8), LANES), :] = jnp.where(
                cd == irrep, held[source].astype(jnp.float32), 0.0
            )
            factor[pl.ds(row, 1), :] = jnp.where(ab_row == irrep, sign / (energy - ab_energy[...]), 0.0)
        return carry

    lax.fori_loop(0, TILES, mask_tile, 0)

    for copy in first:
        copy.wait_recv()

    second_lo, second_hi = [], []
    for k in range(1, NY):
        copy = remote(lo.at[core, y], lo.at[core, y], n, at(dy=k))
        copy.start()
        sends.append(copy)
        second_lo.append(((y - k + NY) % NY, n, at(dy=k)))
        n += 1
    for k in range(1, NZ):
        copy = remote(hi.at[core, z], hi.at[core, z], n, at(dz=k))
        copy.start()
        sends.append(copy)
        second_hi.append(((z - k + NZ) % NZ, n, at(dz=k)))
        n += 1

    forwards = []

    def forward(ref, index):
        nonlocal n
        copy = remote(ref.at[core, index], ref.at[core, index], n, at(dc=1))
        copy.start()
        sends.append(copy)
        forwards.append(remote(ref.at[core, index], ref.at[1 - core, index], n, at(dc=1)))
        n += 1

    forward(lo, y)
    forward(hi, z)

    def regroup(s, carry):
        for c in range(2):
            piece = spread[pl.ds(s * 2 + c, ROWS, stride=PITCH), :]
            rows[s, :, c * LANES:(c + 1) * LANES] = piece.astype(jnp.bfloat16)
        return carry

    lax.fori_loop(0, NY * NZ * NCORE, regroup, 0)

    order = []
    for k in range(1, NY):
        order.append((lo, *second_lo[k - 1]))
        if k % 2 == 0:
            order.append((hi, *second_hi[k // 2 - 1]))
    for ref, index, number, peer in order:
        remote(ref.at[core, index], ref.at[core, index], number, peer).wait_recv()
        forward(ref, index)
    for copy in forwards:
        copy.wait_recv()

    def contract(t, total):
        for s in range(NZ * NCORE):
            zz, cc = s // NCORE, s % NCORE
            block = jnp.concatenate([lo[cc, t, zz], hi[cc, zz, t]], axis=0)
            total = total + lax.dot_general(
                block, rows[t * (NZ * NCORE) + s], NT, preferred_element_type=jnp.float32
            )
        return total

    total = lax.fori_loop(0, NY, contract, jnp.zeros((WIDTH, ROWS), jnp.float32))

    over_x[x] = jnp.zeros((WIDTH, LANES), jnp.float32)
    over_x[x, :, :ROWS] = total * (0.5 * sign)
    arrivals = []
    for k in range(1, NX):
        copy = remote(over_x.at[x], over_x.at[x], n, at(dx=k))
        copy.start()
        sends.append(copy)
        arrivals.append(remote(over_x.at[x], over_x.at[(x - k + NX) % NX], n, at(dx=k)))
        n += 1
    for copy in arrivals:
        copy.wait_recv()
    total = over_x[0]
    for k in range(1, NX):
        total = total + over_x[k]
    mine = mirror * NH + half
    over_m[mine] = total
    arrivals = []
    for m, h in ((0, 1), (1, 0), (1, 1)):
        peer = at(dy=m * (NY // 2), dh=h)
        theirs = ((mirror + m) % 2) * NH + (half + h) % NH
        copy = remote(over_m.at[mine], over_m.at[mine], n, peer)
        copy.start()
        sends.append(copy)
        arrivals.append(remote(over_m.at[mine], over_m.at[theirs], n, peer))
        n += 1
    for copy in arrivals:
        copy.wait_recv()
    total = (over_m[0] + over_m[1]) + (over_m[2] + over_m[3])

    full = lax.dot_general(
        total, pick, TN, preferred_element_type=jnp.float32, precision=lax.Precision.HIGHEST
    )
    result[...] = full[:ROWS] * factor[...]
    for r in range(ROWS):
        q = r % (OB * OB)
        source = r + mirror * ((q % OB) * OB + q // OB - q)
        out[r:r + 1, :] = result[pl.ds(source, 1), :]
    for copy in sends:
        copy.wait_send()


N_COPIES = 10 + 10 + 12 + 7 + 3


def one_pass(chunk, collective_id, arrays):
    smem = pl.BlockSpec(memory_space=pltpu.SMEM)
    vmem = pl.BlockSpec(memory_space=pltpu.VMEM)
    return pl.pallas_call(
        kernel,
        out_shape=(
            jax.ShapeDtypeStruct((ROWS, LANES), jnp.float32),
            jax.ShapeDtypeStruct((8, LANES), jnp.int32),
        ),
        in_specs=[smem] * 5 + [pl.BlockSpec(memory_space=pl.ANY)] + [vmem] * 5,
        out_specs=(vmem, vmem),
        scratch_shapes=[
            pltpu.VMEM((ROWS, LANES, LANES), jnp.bfloat16),
            pltpu.VMEM((ROWS * PITCH, LANES), jnp.float32),
            pltpu.VMEM((NY * NZ * NCORE, ROWS, 2 * LANES), jnp.bfloat16),
            pltpu.VMEM((NCORE, NY, NZ, HALF, 2 * LANES), jnp.bfloat16),
            pltpu.VMEM((NCORE, NZ, NY, HALF, 2 * LANES), jnp.bfloat16),
            pltpu.VMEM((ROWS, LANES), jnp.float32),
            pltpu.VMEM((NX, WIDTH, LANES), jnp.float32),
            pltpu.VMEM((2 * NH, WIDTH, LANES), jnp.float32),
            pltpu.VMEM((ROWS, LANES), jnp.float32),
            pltpu.SemaphoreType.DMA,
            pltpu.SemaphoreType.DMA((N_COPIES,)),
            pltpu.SemaphoreType.DMA((N_COPIES,)),
        ],
        compiler_params=pltpu.CompilerParams(
            collective_id=collective_id, has_side_effects=True, vmem_limit_bytes=56 * 2**20
        ),
        cost_estimate=pl.CostEstimate(
            flops=2 * ROWS * WIDTH * LANES * LANES, bytes_accessed=2 * ROWS * LANES * LANES, transcendentals=0
        ),
        name="ladder",
    )(*arrays[:4], chunk, *arrays[4:])


def on_device(
    amplitudes, integrals, tile_blocks, occ_irrep, slab_irrep, virt_irrep, ab_irrep, occ_energy, ab_energy
):
    row = lambda vector: vector.reshape(1, LANES)
    arrays = (
        tile_blocks, occ_irrep, slab_irrep, occ_energy,
        amplitudes.reshape(ROWS, LANES, LANES), integrals,
        row(virt_irrep), row(slab_irrep), row(ab_irrep), row(ab_energy),
    )
    update, top = one_pass(jnp.zeros((1,), jnp.int32), 0, arrays)
    last = top[0, 0]

    def again(state):
        chunk, so_far = state
        more, _ = one_pass(chunk.reshape(1), 1, arrays)
        return chunk + 1, so_far + more

    _, update = lax.while_loop(lambda state: state[0] * WIDTH <= last, again, (jnp.int32(1), update))
    return update.reshape(TILES, OB * OB, LANES)


def solution(mesh):
    return jax.shard_map(
        on_device,
        mesh=mesh,
        in_specs=(
            P("pair", None, None, "virt"), P("pair", "virt", None), P("pair", None),
            P(), P(), P("virt"), P(), P(), P(),
        ),
        out_specs=P("pair", None, None),
        check_vma=False,
    )
```

time: 265 us -> 58.5 us (0.22)
  the two profiles are of different devices: /device:TPU:16 before, /device:TPU:1 now
where the time goes in v1:
time: 58.5 us; the launch traced here: 58.4 us
  Pallas kernels  54.8 us (94%)
  local copies, waits for them, and re-layouts  2.81 us (5%)
  loops' own time  0.64 us (1%)
    pallas_call x1, Pallas kernels, one_pass(): pl.pallas_call(kernel, out_shape=(jax.ShapeDtypeStruct((ROWS, LANES), jnp...  54.8 us
    unnamed x18, local copies, waits for them, and re-layouts  1.58 us
    slice x1, local copies, waits for them, and re-layouts, on_device(): last = top[0, 0]  1.23 us

profile of v1, /device:TPU:1, one launch (start us, length us, event | category | flops | bytes accessed | tf_op | source)
XLA Modules:
  0.0 58.4 jit_solution(9030788696108744268)
XLA Ops:
  0.0 0.0 copy-start.2
  0.0 0.0 copy-start.4
  0.0 0.0 copy-start.3
  0.0 0.0 copy-start.1
  0.0 0.0 copy-start.7
  0.0 0.0 copy-start.6
  0.0 0.0 copy-start.5
  0.1 0.0 copy-start
  0.1 0.9 %copy.10.tile_blocks = s32[6,2]{1,0:T(8,128)S(1)} copy(s32[6,2]{0,1:T(2,128)} %param.13) | data formatting | bytes 96 | tf_op args[2]
  1.0 54.8 %ladder.2 = (f32[96,128]{1,0:T(8,128)S(1)}, s32[8,128]{1,0:T(8,128)}) custom-call(s32[6,2]{1,0:T(8,128)S(1)} %copy.10.tile_blocks, s32[128]{0:T(128)} %occ_irrep.1, s32[128]{0:T(128)} %slab_scalar.1, f32[128]{0:T(128)} %occ_energy.1, s32[1]{0:T(128)} %constant.4.clone.1.chunk, bf16[96,128,128]{2,1,0:T(8,128)(2,1)} %bitcast.10, bf16[2,128,128]{2,1,0:T(8,128)(2,1)} %ints.1, ...), custom_call_target="tpu_custom_call" | custom-call | flops 100663296 | bytes 3145728 | tf_op jit(solution)/shard_map/ladder/pallas_call | solution.py:221
  55.8 1.2 %slice.3 = s32[1,1]{1,0:T(1,128)} slice(s32[8,128]{1,0:T(8,128)} %get-tuple-element.77), slice={[0:1], [0:1]} | slice | bytes 8 | tf_op jit(solution)/shard_map/slice | solution.py:263
  57.0 0.0 copy-done.2
  57.0 0.0 copy-done.4
  57.0 0.0 copy-done.3
  57.0 0.0 copy-done.1
  57.0 0.0 copy-done.7
  57.1 0.0 copy-done.6
  57.1 0.0 copy-done.5
  57.1 0.0 copy-done
  57.1 0.6 %while.10 = (s32[]{:T(128)}, f32[96,128]{1,0:T(8,128)S(1)}, s32[]{:T(128)}, s32[6,2]{1,0:T(8,128)S(1)}, s32[128]{0:T(128)S(1)}, /*index=5*/s32[128]{0:T(128)S(1)...) while((s32[]{:T(128)}, f32[96,128]{1,0:T(8,128)S(1)}, ...), condition=%wide.region_1.0_spmd, body=%wide.region_0.0_spmd.sunk | while | flops 100675584 | bytes 3293337 | solution.py:270
  57.7 0.6 %copy.19 = f32[6,16,128]{2,1,0:T(8,128)} copy(f32[6,16,128]{2,1,0:T(8,128)S(1)} %bitcast.12) | data formatting | bytes 98304
Async XLA Ops:
  0.0 57.0 %copy-start.2 = (s32[128]{0:T(128)S(1)}, s32[128]{0:T(128)}, u32[]{:S(2)}) copy-start(s32[128]{0:T(128)} %slab_scalar.1) | copy-start | bytes 1540
  0.0 57.0 %copy-start.4 = (f32[128]{0:T(128)S(1)}, f32[128]{0:T(128)}, u32[]{:S(2)}) copy-start(f32[128]{0:T(128)} %occ_energy.1) | copy-start | bytes 1540
  0.0 57.0 %copy-start.3 = (s32[128]{0:T(128)S(1)}, s32[128]{0:T(128)}, u32[]{:S(2)}) copy-start(s32[128]{0:T(128)} %occ_irrep.1) | copy-start | bytes 1540
  0.0 57.0 %copy-start.1 = (bf16[2,128,128]{2,1,0:T(8,128)(2,1)S(1)}, bf16[2,128,128]{2,1,0:T(8,128)(2,1)}, u32[]{:S(2)}) copy-start(bf16[2,128,128]{2,1,0:T(8,128)(2,1)} %ints.1) | copy-start | bytes 196612
  0.0 57.0 %copy-start.7 = (f32[128]{0:T(128)S(1)}, f32[128]{0:T(128)}, u32[]{:S(2)}) copy-start(f32[128]{0:T(128)} %param.19) | copy-start | bytes 1540
  0.0 57.0 %copy-start.6 = (s32[128]{0:T(128)S(1)}, s32[128]{0:T(128)}, u32[]{:S(2)}) copy-start(s32[128]{0:T(128)} %param.17) | copy-start | bytes 1540
  0.0 57.0 %copy-start.5 = (s32[128]{0:T(128)S(1)}, s32[128]{0:T(128)}, u32[]{:S(2)}) copy-start(s32[128]{0:T(128)} %param.16) | copy-start | bytes 1540
  0.1 57.0 %copy-start = (bf16[6,16,128,128]{3,2,1,0:T(8,128)(2,1)S(1)}, bf16[6,16,128,128]{3,2,1,0:T(8,128)(2,1)}, u32[]{:S(2)}) copy-start(bf16[6,16,128,128]{3,2,1,0:T(8,128)(2,1)} %param.11) | copy-start | bytes 9437188

commit v2 on v1

v2 whole, which is shorter than its diff:
```python
import functools

import jax
import jax.numpy as jnp
from jax import lax
from jax.experimental import pallas as pl
from jax.experimental.pallas import tpu as pltpu
from jax.sharding import PartitionSpec as P

OB = 4
TILES = 6
ROWS = TILES * OB * OB
LANES = 128
WIDTH = 32
HALF = WIDTH // 2
NY, NZ, NCORE, NX, NH = 8, 4, 2, 8, 2
PITCH = 136
FAR_FIRST = (4, 3, 5, 2, 6, 1, 7)
NEAR_FIRST = FAR_FIRST[::-1]
MESH = pl.DeviceIdType.MESH
NT = (((1,), (1,)), ((), ()))
TN = (((0,), (0,)), ((), ()))


def place():
    pair, virt = lax.axis_index("pair"), lax.axis_index("virt")
    return pair // (NZ * NCORE), (pair // NCORE) % NZ, pair % NCORE, virt // NX, virt % NX


def kernel(
    tile_blocks_in, occ_irrep_in, slab_in, occ_energy_in, amps, ints_in, virt_in, slab_row_in, ab_in, ab_energy_in,
    *refs,
):
    chunk_in = refs[0] if len(refs) == 26 else None
    (
        out, top, tile_blocks, occ_irrep, slab_scalar, occ_energy, ints, virt, slab, ab, ab_energy, chunk,
        held, spread, rows, lo, hi, factor, over_x, over_m, result, sem_in, send, recv, ready,
    ) = refs[-25:]
    y, z, core, half, x = place()
    mirror = y // (NY // 2)

    def at(dy=0, dz=0, dc=0, dh=0, dx=0):
        pair = ((y + dy) % NY) * (NZ * NCORE) + ((z + dz) % NZ) * NCORE + (core + dc) % NCORE
        return pair, ((half + dh) % NH) * NX + (x + dx) % NX

    peers = [at(dy=k) for k in FAR_FIRST] + [at(dh=1)] + [at(dx=k) for k in FAR_FIRST]
    peers += [at(dz=k) for k in range(1, NZ)] + [at(dc=1)]
    barrier = pltpu.get_barrier_semaphore()
    for peer in peers:
        pl.semaphore_signal(barrier, inc=1, device_id=peer, device_id_type=MESH)

    loads = []
    for source, target in (
        (ab_in, ab), (virt_in, virt), (slab_in, slab_scalar), (ints_in, ints),
        (tile_blocks_in, tile_blocks), (occ_irrep_in, occ_irrep), (occ_energy_in, occ_energy),
        (slab_row_in, slab), (ab_energy_in, ab_energy), (amps, held), (chunk_in, chunk),
    ):
        if source is None:
            continue
        copy = pltpu.make_async_copy(source, target, sem_in.at[len(loads)])
        copy.start()
        loads.append(copy)
    for copy in loads[:4] + loads[10:]:
        copy.wait()

    def remote(src, dst, number, peer):
        return pltpu.make_async_remote_copy(
            src_ref=src, dst_ref=dst, send_sem=send.at[number], recv_sem=recv.at[number],
            device_id=peer, device_id_type=MESH,
        )

    ab_row = ab[...].reshape(1, LANES)
    ab_rows = jnp.broadcast_to(ab_row, (LANES, LANES))
    ab_cols = jnp.transpose(ab_rows)
    before = lax.broadcasted_iota(jnp.int32, (LANES, LANES), 0) < lax.broadcasted_iota(jnp.int32, (LANES, LANES), 1)
    same = jnp.where((ab_rows == ab_cols) & before, 1.0, 0.0)
    rank = jnp.sum(same, axis=0, keepdims=True).astype(jnp.int32)
    top[0] = jnp.max(rank)
    slot = lax.broadcasted_iota(jnp.int32, (WIDTH, LANES), 0)
    if chunk_in is not None:
        slot = slot + chunk[...] * WIDTH
    pick = jnp.where(slot == jnp.broadcast_to(rank, (WIDTH, LANES)), 1.0, 0.0)
    pick_narrow = pick.astype(jnp.bfloat16)
    virt_rows = jnp.broadcast_to(virt[...], (LANES, LANES))
    virt_cols = jnp.transpose(virt_rows)
    labels = jnp.bitwise_xor(virt_cols, ab_rows)
    own = (y * NZ + z) * NCORE + core
    for c in range(2):
        kept = jnp.where(labels == slab_scalar[own * 2 + c], ints[c].astype(jnp.float32), 0.0).astype(jnp.bfloat16)
        packed = lax.dot_general(pick_narrow, kept, NT, preferred_element_type=jnp.float32).astype(jnp.bfloat16)
        lo[core, y, z, :, c * LANES:(c + 1) * LANES] = packed[:HALF]
        hi[core, z, y, :, c * LANES:(c + 1) * LANES] = packed[HALF:]

    pl.semaphore_wait(barrier, len(peers))
    pl.semaphore_signal(ready, inc=1, device_id=at(dy=NY // 2), device_id_type=MESH)

    sends = []

    def push(ref, peer):
        number = len(sends)
        copy = remote(ref, ref, number, peer)
        copy.start()
        sends.append(copy)
        return lambda arriving: remote(arriving, arriving, number, peer).wait_recv()

    first_lo = {k: push(lo.at[core, y, z], at(dz=k)) for k in range(1, NZ)}
    first_hi = {k: push(hi.at[core, z, y], at(dy=k)) for k in FAR_FIRST}

    for copy in loads[4:10]:
        copy.wait()
    cd = jnp.bitwise_xor(jnp.transpose(jnp.broadcast_to(slab[...], (LANES, LANES))), virt_rows)
    sign = (1 - 2 * mirror).astype(jnp.float32)

    def mask_tile(k, carry):
        for q in range(OB * OB):
            i, j = q // OB, q % OB
            source = k * (OB * OB) + q + mirror * (j * OB + i - q)
            a = tile_blocks[0, k] * OB + (i + mirror * (j - i))
            b = tile_blocks[1, k] * OB + (j + mirror * (i - j))
            irrep = jnp.bitwise_xor(occ_irrep[a], occ_irrep[b])
            energy = occ_energy[a] + occ_energy[b]
            row = k * (OB * OB) + q
            spread[pl.ds(pl.multiple_of(row * PITCH, 8), LANES), :] = jnp.where(
                cd == irrep, held[source].astype(jnp.float32), 0.0
            )
            factor[pl.ds(row, 1), :] = jnp.where(ab_row == irrep, sign / (energy - ab_energy[...]), 0.0)
        return carry

    lax.fori_loop(0, TILES, mask_tile, 0)

    for k, arrived in first_lo.items():
        arrived(lo.at[core, y, (z - k + NZ) % NZ])
    second_lo = {k: push(lo.at[core, y], at(dy=k)) for k in FAR_FIRST}
    for k, arrived in first_hi.items():
        arrived(hi.at[core, z, (y - k + NY) % NY])
    second_hi = {k: push(hi.at[core, z], at(dz=k)) for k in range(1, NZ)}
    sibling_lo = {0: push(lo.at[core, y], at(dc=1))}
    sibling_hi = {0: push(hi.at[core, z], at(dc=1))}

    def regroup(s, carry):
        for c in range(2):
            piece = spread[pl.ds(s * 2 + c, ROWS, stride=PITCH), :]
            rows[s, :, c * LANES:(c + 1) * LANES] = piece.astype(jnp.bfloat16)
        return carry

    lax.fori_loop(0, NY * NZ * NCORE, regroup, 0)

    def contract(total, c, slab_y):
        for zz in range(NZ):
            block = jnp.concatenate([lo[c, slab_y, zz], hi[c, zz, slab_y]], axis=0)
            total = total + lax.dot_general(
                block, rows[(slab_y * NZ + zz) * NCORE + c], NT, preferred_element_type=jnp.float32
            )
        return total

    for k, arrived in second_hi.items():
        source = hi.at[core, (z - k + NZ) % NZ]
        arrived(source)
        sibling_hi[k] = push(source, at(dc=1))
    total = contract(jnp.zeros((WIDTH, ROWS), jnp.float32), core, y)
    for k in NEAR_FIRST:
        slab_y = (y - k + NY) % NY
        source = lo.at[core, slab_y]
        second_lo[k](source)
        sibling_lo[k] = push(source, at(dc=1))
        total = contract(total, core, slab_y)
    for k, arrived in sibling_hi.items():
        arrived(hi.at[1 - core, (z - k + NZ) % NZ])
    for k, arrived in sibling_lo.items():
        slab_y = (y - k + NY) % NY
        arrived(lo.at[1 - core, slab_y])
        total = contract(total, 1 - core, slab_y)

    over_x[x] = jnp.zeros((WIDTH, LANES), jnp.float32)
    over_x[x, :, :ROWS] = total * (0.5 * sign)
    arrivals = {k: push(over_x.at[x], at(dx=k)) for k in FAR_FIRST}
    for k, arrived in arrivals.items():
        arrived(over_x.at[(x - k + NX) % NX])
    total = over_x[0]
    for k in range(1, NX):
        total = total + over_x[k]
    mine = mirror * NH + half
    over_m[mine] = total
    pl.semaphore_wait(ready, 1)
    arrivals = {
        (m, h): push(over_m.at[mine], at(dy=m * (NY // 2), dh=h)) for m, h in ((1, 1), (0, 1), (1, 0))
    }
    for (m, h), arrived in arrivals.items():
        arrived(over_m.at[((mirror + m) % 2) * NH + (half + h) % NH])
    total = (over_m[0] + over_m[1]) + (over_m[2] + over_m[3])

    full = lax.dot_general(
        total, pick, TN, preferred_element_type=jnp.float32, precision=lax.Precision.HIGHEST
    )
    result[...] = full[:ROWS] * factor[...]
    for r in range(ROWS):
        q = r % (OB * OB)
        source = r + mirror * ((q % OB) * OB + q // OB - q)
        out[r:r + 1, :] = result[pl.ds(source, 1), :]
    for copy in sends:
        copy.wait_send()


N_COPIES = 10 + 10 + 12 + 7 + 3


def one_pass(collective_id, arrays):
    smem = pl.BlockSpec(memory_space=pltpu.SMEM)
    vmem = pl.BlockSpec(memory_space=pltpu.VMEM)
    return pl.pallas_call(
        kernel,
        out_shape=(
            jax.ShapeDtypeStruct((ROWS, LANES), jnp.float32),
            jax.ShapeDtypeStruct((1,), jnp.int32),
        ),
        in_specs=[pl.BlockSpec(memory_space=pl.ANY)] * len(arrays),
        out_specs=(vmem, smem),
        scratch_shapes=[
            pltpu.SMEM((2, TILES), jnp.int32),
            pltpu.SMEM((LANES,), jnp.int32),
            pltpu.SMEM((LANES,), jnp.int32),
            pltpu.SMEM((LANES,), jnp.float32),
            pltpu.VMEM((2, LANES, LANES), jnp.bfloat16),
            pltpu.VMEM((1, LANES), jnp.int32),
            pltpu.VMEM((1, LANES), jnp.int32),
            pltpu.VMEM((1, LANES), jnp.int32),
            pltpu.VMEM((1, LANES), jnp.float32),
            pltpu.VMEM((1, LANES), jnp.int32),
            pltpu.VMEM((ROWS, LANES, LANES), jnp.bfloat16),
            pltpu.VMEM((ROWS * PITCH, LANES), jnp.float32),
            pltpu.VMEM((NY * NZ * NCORE, ROWS, 2 * LANES), jnp.bfloat16),
            pltpu.VMEM((NCORE, NY, NZ, HALF, 2 * LANES), jnp.bfloat16),
            pltpu.VMEM((NCORE, NZ, NY, HALF, 2 * LANES), jnp.bfloat16),
            pltpu.VMEM((ROWS, LANES), jnp.float32),
            pltpu.VMEM((NX, WIDTH, LANES), jnp.float32),
            pltpu.VMEM((2 * NH, WIDTH, LANES), jnp.float32),
            pltpu.VMEM((ROWS, LANES), jnp.float32),
            pltpu.SemaphoreType.DMA((11,)),
            pltpu.SemaphoreType.DMA((N_COPIES,)),
            pltpu.SemaphoreType.DMA((N_COPIES,)),
            pltpu.SemaphoreType.REGULAR,
        ],
        compiler_params=pltpu.CompilerParams(
            collective_id=collective_id, has_side_effects=True, vmem_limit_bytes=56 * 2**20
        ),
        cost_estimate=pl.CostEstimate(
            flops=2 * ROWS * WIDTH * LANES * LANES, bytes_accessed=2 * ROWS * LANES * LANES, transcendentals=0
        ),
        name="ladder",
    )(*arrays)


def on_device(
    amplitudes, integrals, tile_blocks, occ_irrep, slab_irrep, virt_irrep, ab_irrep, occ_energy, ab_energy
):
    row = lambda vector: vector.reshape(1, LANES)
    arrays = (
        tile_blocks.T, occ_irrep, slab_irrep, occ_energy,
        amplitudes.reshape(ROWS, LANES, LANES), integrals, row(virt_irrep), row(slab_irrep),
        row(ab_irrep), row(ab_energy),
    )
    update, top = one_pass(0, arrays)

    def again(state):
        chunk, so_far = state
        more, _ = one_pass(1, (*arrays, jnp.full((1, LANES), chunk)))
        return chunk + 1, so_far + more

    _, update = lax.while_loop(lambda state: state[0] * WIDTH <= top[0], again, (jnp.int32(1), update))
    return update.reshape(TILES, OB * OB, LANES)


def solution(mesh):
    return jax.shard_map(
        on_device,
        mesh=mesh,
        in_specs=(
            P("pair", None, None, "virt"), P("pair", "virt", None), P("pair", None),
            P(), P(), P("virt"), P(), P(), P(),
        ),
        out_specs=P("pair", None, None),
        check_vma=False,
    )
```

time: 58.5 us -> 51.3 us (0.88)
  Pallas kernels: 54.8 us -> 49.7 us
  local copies, waits for them, and re-layouts: 2.81 us -> 0.66 us
    pallas_call x1, Pallas kernels: 54.8 us -> 49.7 us  [one_pass(): pl.pallas_call(kernel, out_shape=(jax.ShapeDtypeStruct((ROWS, LANES), jnp...]
    slice x1 -> x0, local copies, waits for them, and re-layouts: 1.23 us -> none  [on_device(): last = top[0, 0]]
    unnamed x18 -> x19, local copies, waits for them, and re-layouts: 1.58 us -> 0.66 us
where the time goes in v2:
time: 51.3 us; the launch traced here: 51.1 us
  Pallas kernels  49.7 us (97%)
  local copies, waits for them, and re-layouts  0.66 us (1%)
  loops' own time  0.64 us (1%)
    pallas_call x1, Pallas kernels, one_pass(): pl.pallas_call(kernel, out_shape=(jax.ShapeDtypeStruct((ROWS, LANES), jnp...  49.7 us

profile of v2, /device:TPU:1, one launch (start us, length us, event | category | flops | bytes accessed | tf_op | source)
XLA Modules:
  0.0 51.1 jit_solution(2147056500579691950)
XLA Ops:
  0.0 0.0 copy-start.2
  0.0 0.0 copy-start.5
  0.0 0.0 copy-start.4
  0.0 0.0 copy-start.1
  0.0 0.0 copy-start.8
  0.0 0.0 copy-start.7
  0.0 0.0 copy-start.6
  0.0 0.0 copy-start.3
  0.1 0.0 copy-start
  0.1 49.7 %ladder.2 = (f32[96,128]{1,0:T(8,128)S(1)}, s32[1]{0:T(128)}) custom-call(s32[2,6]{1,0:T(2,128)} %bitcast.16, s32[128]{0:T(128)} %occ_irrep_in.1, s32[128]{0:T(128)} %slab_in.1, f32[128]{0:T(128)} %occ_energy_in.1, bf16[96,128,128]{2,1,0:T(8,128)(2,1)} %bitcast.9, bf16[2,128,128]{2,1,0:T(8,128)(2,1)} %ints_in.1, s32[1,128]{1,0:T(1,128)} %bitcast.18, ...), custom_call_target="tpu_custom_call" | custom-call | flops 100663296 | bytes 3145728 | tf_op jit(solution)/shard_map/ladder/pallas_call | solution.py:210
  49.8 0.0 copy-done.2
  49.8 0.0 copy-done.5
  49.8 0.0 copy-done.4
  49.8 0.0 copy-done.1
  49.8 0.0 copy-done.8
  49.8 0.0 copy-done.7
  49.8 0.0 copy-done.6
  49.9 0.0 copy-done.3
  49.9 0.0 copy-done
  49.9 0.6 %while.10 = (s32[]{:T(128)}, f32[96,128]{1,0:T(8,128)S(1)}, s32[1]{0:T(128)}, s32[2,6]{1,0:T(2,128)S(1)}, s32[128]{0:T(128)S(1)}, /*index=5*/s32[128]{0:T(128)S(...) while((s32[]{:T(128)}, f32[96,128]{1,0:T(8,128)S(1)}, ...), condition=%wide.region_1.0_spmd, body=%wide.region_0.0_spmd.sunk | while | flops 100675584 | bytes 3293853 | solution.py:269
  50.5 0.6 %copy.17 = f32[6,16,128]{2,1,0:T(8,128)} copy(f32[6,16,128]{2,1,0:T(8,128)S(1)} %bitcast.11) | data formatting | bytes 98304
Async XLA Ops:
  0.0 49.8 %copy-start.2 = (s32[128]{0:T(128)S(1)}, s32[128]{0:T(128)}, u32[]{:S(2)}) copy-start(s32[128]{0:T(128)} %slab_in.1) | copy-start | bytes 1540
  0.0 49.8 %copy-start.5 = (f32[128]{0:T(128)S(1)}, f32[128]{0:T(128)}, u32[]{:S(2)}) copy-start(f32[128]{0:T(128)} %occ_energy_in.1) | copy-start | bytes 1540
  0.0 49.8 %copy-start.4 = (s32[128]{0:T(128)S(1)}, s32[128]{0:T(128)}, u32[]{:S(2)}) copy-start(s32[128]{0:T(128)} %occ_irrep_in.1) | copy-start | bytes 1540
  0.0 49.8 %copy-start.1 = (bf16[2,128,128]{2,1,0:T(8,128)(2,1)S(1)}, bf16[2,128,128]{2,1,0:T(8,128)(2,1)}, u32[]{:S(2)}) copy-start(bf16[2,128,128]{2,1,0:T(8,128)(2,1)} %ints_in.1) | copy-start | bytes 196612
  0.0 49.8 %copy-start.8 = (f32[128]{0:T(128)S(1)}, f32[128]{0:T(128)}, u32[]{:S(2)}) copy-start(f32[128]{0:T(128)} %param.19) | copy-start | bytes 1540
  0.0 49.8 %copy-start.7 = (s32[128]{0:T(128)S(1)}, s32[128]{0:T(128)}, u32[]{:S(2)}) copy-start(s32[128]{0:T(128)} %param.17) | copy-start | bytes 1540
  0.0 49.8 %copy-start.6 = (s32[128]{0:T(128)S(1)}, s32[128]{0:T(128)}, u32[]{:S(2)}) copy-start(s32[128]{0:T(128)} %param.16) | copy-start | bytes 1540
  0.0 49.8 %copy-start.3 = (s32[6,2]{0,1:T(2,128)S(1)}, s32[6,2]{0,1:T(2,128)}, u32[]{:S(2)}) copy-start(s32[6,2]{0,1:T(2,128)} %param.13) | copy-start | bytes 148
  0.1 49.8 %copy-start = (bf16[6,16,128,128]{3,2,1,0:T(8,128)(2,1)S(1)}, bf16[6,16,128,128]{3,2,1,0:T(8,128)(2,1)}, u32[]{:S(2)}) copy-start(bf16[6,16,128,128]{3,2,1,0:T(8,128)(2,1)} %param.11) | copy-start | bytes 9437188

commit v3 on v2

--- a/solution.py
+++ b/solution.py
@@ -31,23 +31,30 @@
     tile_blocks_in, occ_irrep_in, slab_in, occ_energy_in, amps, ints_in, virt_in, slab_row_in, ab_in, ab_energy_in,
     *refs,
 ):
-    chunk_in = refs[0] if len(refs) == 26 else None
+    chunk_in = refs[0] if len(refs) == 27 else None
     (
         out, top, tile_blocks, occ_irrep, slab_scalar, occ_energy, ints, virt, slab, ab, ab_energy, chunk,
-        held, spread, rows, lo, hi, factor, over_x, over_m, result, sem_in, send, recv, ready,
-    ) = refs[-25:]
+        held, spread, rows, blocks, factor, over_x, over_m, result, sem_in, send, recv, ready, across, above,
+    ) = refs[-26:]
     y, z, core, half, x = place()
     mirror = y // (NY // 2)
 
     def at(dy=0, dz=0, dc=0, dh=0, dx=0):
-        pair = ((y + dy) % NY) * (NZ * NCORE) + ((z + dz) % NZ) * NCORE + (core + dc) % NCORE
+        pair = ((y + dy) % NY) * (NZ * NCORE) + ((z + dz + NZ) % NZ) * NCORE + (core + dc) % NCORE
         return pair, ((half + dh) % NH) * NX + (x + dx) % NX
 
-    peers = [at(dy=k) for k in FAR_FIRST] + [at(dh=1)] + [at(dx=k) for k in FAR_FIRST]
-    peers += [at(dz=k) for k in range(1, NZ)] + [at(dc=1)]
+    peers = [at(dy=k) for k in FAR_FIRST] + [at(dx=k) for k in FAR_FIRST] + [at(dc=1)]
     barrier = pltpu.get_barrier_semaphore()
     for peer in peers:
         pl.semaphore_signal(barrier, inc=1, device_id=peer, device_id_type=MESH)
+    for k in range(1, NZ):
+        @pl.when(z + k < NZ)
+        def _():
+            pl.semaphore_signal(barrier, inc=1, device_id=at(dz=k), device_id_type=MESH)
+
+    @pl.when(half == 0)
+    def _():
+        pl.semaphore_signal(barrier, inc=1, device_id=at(dh=1), device_id_type=MESH)
 
     loads = []
     for source, target in (
@@ -88,23 +95,40 @@
     for c in range(2):
         kept = jnp.where(labels == slab_scalar[own * 2 + c], ints[c].astype(jnp.float32), 0.0).astype(jnp.bfloat16)
         packed = lax.dot_general(pick_narrow, kept, NT, preferred_element_type=jnp.float32).astype(jnp.bfloat16)
-        lo[core, y, z, :, c * LANES:(c + 1) * LANES] = packed[:HALF]
-        hi[core, z, y, :, c * LANES:(c + 1) * LANES] = packed[HALF:]
-
-    pl.semaphore_wait(barrier, len(peers))
-    pl.semaphore_signal(ready, inc=1, device_id=at(dy=NY // 2), device_id_type=MESH)
+        for h in range(2):
+            blocks[core, 0, 0, h, :, c * LANES:(c + 1) * LANES] = packed[h * HALF:(h + 1) * HALF]
+
+    pl.semaphore_wait(barrier, len(peers) + z + half)
+    for k in range(1, NZ):
+        @pl.when(z >= k)
+        def _():
+            pl.semaphore_signal(above.at[k], inc=1, device_id=at(dz=-k), device_id_type=MESH)
+
+    def ready_for_mirror():
+        pl.semaphore_signal(ready, inc=1, device_id=at(dy=NY // 2), device_id_type=MESH)
+
+    @pl.when(half == 1)
+    def _():
+        pl.semaphore_signal(across, inc=1, device_id=at(dh=1), device_id_type=MESH)
+        ready_for_mirror()
 
     sends = []
 
-    def push(ref, peer):
-        number = len(sends)
-        copy = remote(ref, ref, number, peer)
-        copy.start()
+    def push(source, target, peer, start=True):
+        copy = remote(source, target, len(sends), peer)
+        if start:
+            copy.start()
         sends.append(copy)
-        return lambda arriving: remote(arriving, arriving, number, peer).wait_recv()
-
-    first_lo = {k: push(lo.at[core, y, z], at(dz=k)) for k in range(1, NZ)}
-    first_hi = {k: push(hi.at[core, z, y], at(dy=k)) for k in FAR_FIRST}
+        return copy
+
+    own_block = blocks.at[core, 0, 0]
+    near_z = {k: push(own_block, blocks.at[core, 0, k], at(dz=k), start=False) for k in range(1, NZ)}
+    for k, copy in near_z.items():
+        @pl.when(z + k >= NZ)
+        def _():
+            copy.start()
+
+    near_y = [push(own_block, blocks.at[core, k, 0], at(dy=k)) for k in FAR_FIRST]
 
     for copy in loads[4:10]:
         copy.wait()
@@ -128,15 +152,6 @@
 
     lax.fori_loop(0, TILES, mask_tile, 0)
 
-    for k, arrived in first_lo.items():
-        arrived(lo.at[core, y, (z - k + NZ) % NZ])
-    second_lo = {k: push(lo.at[core, y], at(dy=k)) for k in FAR_FIRST}
-    for k, arrived in first_hi.items():
-        arrived(hi.at[core, z, (y - k + NY) % NY])
-    second_hi = {k: push(hi.at[core, z], at(dz=k)) for k in range(1, NZ)}
-    sibling_lo = {0: push(lo.at[core, y], at(dc=1))}
-    sibling_hi = {0: push(hi.at[core, z], at(dc=1))}
-
     def regroup(s, carry):
         for c in range(2):
             piece = spread[pl.ds(s * 2 + c, ROWS, stride=PITCH), :]
@@ -145,58 +160,103 @@
 
     lax.fori_loop(0, NY * NZ * NCORE, regroup, 0)
 
-    def contract(total, c, slab_y):
-        for zz in range(NZ):
-            block = jnp.concatenate([lo[c, slab_y, zz], hi[c, zz, slab_y]], axis=0)
+    for k, copy in near_z.items():
+        @pl.when(z + k < NZ)
+        def _():
+            pl.semaphore_wait(above.at[k], 1)
+            copy.start()
+
+    for copy in near_z.values():
+        copy.wait_recv()
+    far_lo = {
+        k: push(blocks.at[core, 0, pl.ds(1, NZ - 1), 0], blocks.at[core, k, pl.ds(1, NZ - 1), 0], at(dy=k))
+        for k in FAR_FIRST
+    }
+    for copy in near_y:
+        copy.wait_recv()
+    far_hi = {
+        k: push(blocks.at[core, pl.ds(1, NY - 1), 0, 1], blocks.at[core, pl.ds(1, NY - 1), k, 1], at(dz=k))
+        for k in range(1, NZ)
+    }
+
+    def share(part):
+        return push(part, part, at(dc=1))
+
+    shared = [share(blocks.at[core, :, 0]), share(blocks.at[core, 0, pl.ds(1, NZ - 1)])]
+
+    def contract(total, c, ky, kzs):
+        for kz in kzs:
+            source = ((y - ky + NY) % NY * NZ + (z - kz + NZ) % NZ) * NCORE + c
             total = total + lax.dot_general(
-                block, rows[(slab_y * NZ + zz) * NCORE + c], NT, preferred_element_type=jnp.float32
+                blocks[c, ky, kz].reshape(WIDTH, 2 * LANES), rows[source], NT, preferred_element_type=jnp.float32
             )
         return total
 
-    for k, arrived in second_hi.items():
-        source = hi.at[core, (z - k + NZ) % NZ]
-        arrived(source)
-        sibling_hi[k] = push(source, at(dc=1))
-    total = contract(jnp.zeros((WIDTH, ROWS), jnp.float32), core, y)
+    def contract_near(total, c):
+        total = contract(total, c, 0, range(NZ))
+        for ky in range(1, NY):
+            total = contract(total, c, ky, range(1))
+        return total
+
+    total = contract_near(jnp.zeros((WIDTH, ROWS), jnp.float32), core)
+    for copy in shared:
+        copy.wait_recv()
+    total = contract_near(total, 1 - core)
+    shared_hi, shared_lo = [], []
+    for k, copy in far_hi.items():
+        copy.wait_recv()
+        shared_hi.append(share(blocks.at[core, pl.ds(1, NY - 1), k, 1]))
     for k in NEAR_FIRST:
-        slab_y = (y - k + NY) % NY
-        source = lo.at[core, slab_y]
-        second_lo[k](source)
-        sibling_lo[k] = push(source, at(dc=1))
-        total = contract(total, core, slab_y)
-    for k, arrived in sibling_hi.items():
-        arrived(hi.at[1 - core, (z - k + NZ) % NZ])
-    for k, arrived in sibling_lo.items():
-        slab_y = (y - k + NY) % NY
-        arrived(lo.at[1 - core, slab_y])
-        total = contract(total, 1 - core, slab_y)
+        far_lo[k].wait_recv()
+        shared_lo.append(share(blocks.at[core, k, pl.ds(1, NZ - 1), 0]))
+    for k in NEAR_FIRST:
+        total = contract(total, core, k, range(1, NZ))
+    for copy in shared_hi:
+        copy.wait_recv()
+    for k, copy in zip(NEAR_FIRST, shared_lo):
+        copy.wait_recv()
+        total = contract(total, 1 - core, k, range(1, NZ))
+
+    @pl.when(half == 0)
+    def _():
+        pl.semaphore_wait(across, 1)
+        ready_for_mirror()
 
     over_x[x] = jnp.zeros((WIDTH, LANES), jnp.float32)
     over_x[x, :, :ROWS] = total * (0.5 * sign)
-    arrivals = {k: push(over_x.at[x], at(dx=k)) for k in FAR_FIRST}
-    for k, arrived in arrivals.items():
-        arrived(over_x.at[(x - k + NX) % NX])
+    arrivals = [push(over_x.at[x], over_x.at[x], at(dx=k)) for k in FAR_FIRST]
+    for copy in arrivals:
+        copy.wait_recv()
     total = over_x[0]
     for k in range(1, NX):
         total = total + over_x[k]
     mine = mirror * NH + half
     over_m[mine] = total
     pl.semaphore_wait(ready, 1)
-    arrivals = {
-        (m, h): push(over_m.at[mine], at(dy=m * (NY // 2), dh=h)) for m, h in ((1, 1), (0, 1), (1, 0))
-    }
-    for (m, h), arrived in arrivals.items():
-        arrived(over_m.at[((mirror + m) % 2) * NH + (half + h) % NH])
+    arrivals = [
+        push(over_m.at[mine], over_m.at[mine], at(dy=m * (NY // 2), dh=h)) for m, h in ((1, 1), (0, 1), (1, 0))
+    ]
+    for copy in arrivals:
+        copy.wait_recv()
     total = (over_m[0] + over_m[1]) + (over_m[2] + over_m[3])
 
     full = lax.dot_general(
         total, pick, TN, preferred_element_type=jnp.float32, precision=lax.Precision.HIGHEST
     )
-    result[...] = full[:ROWS] * factor[...]
-    for r in range(ROWS):
-        q = r % (OB * OB)
-        source = r + mirror * ((q % OB) * OB + q // OB - q)
-        out[r:r + 1, :] = result[pl.ds(source, 1), :]
+    scaled = full[:ROWS] * factor[...]
+
+    @pl.when(mirror == 0)
+    def _():
+        out[...] = scaled
+
+    @pl.when(mirror == 1)
+    def _():
+        result[...] = scaled
+        for r in range(ROWS):
+            q = r % (OB * OB)
+            source = r + (q % OB) * OB + q // OB - q
+            out[r:r + 1, :] = result[source:source + 1, :]
+
     for copy in sends:
         copy.wait_send()
 
@@ -229,8 +289,7 @@
             pltpu.VMEM((ROWS, LANES, LANES), jnp.bfloat16),
             pltpu.VMEM((ROWS * PITCH, LANES), jnp.float32),
             pltpu.VMEM((NY * NZ * NCORE, ROWS, 2 * LANES), jnp.bfloat16),
-            pltpu.VMEM((NCORE, NY, NZ, HALF, 2 * LANES), jnp.bfloat16),
-            pltpu.VMEM((NCORE, NZ, NY, HALF, 2 * LANES), jnp.bfloat16),
+            pltpu.VMEM((NCORE, NY, NZ, 2, HALF, 2 * LANES), jnp.bfloat16),
             pltpu.VMEM((ROWS, LANES), jnp.float32),
             pltpu.VMEM((NX, WIDTH, LANES), jnp.float32),
             pltpu.VMEM((2 * NH, WIDTH, LANES), jnp.float32),
@@ -239,6 +298,8 @@
             pltpu.SemaphoreType.DMA((N_COPIES,)),
             pltpu.SemaphoreType.DMA((N_COPIES,)),
             pltpu.SemaphoreType.REGULAR,
+            pltpu.SemaphoreType.REGULAR,
+            pltpu.SemaphoreType.REGULAR((NZ,)),
         ],
         compiler_params=pltpu.CompilerParams(
             collective_id=collective_id, has_side_effects=True, vmem_limit_bytes=56 * 2**20

time: 51.3 us -> 51.1 us (level)
  no operation moved by 1% of the time
where the time goes in v3:
time: 51.1 us; the launch traced here: 50.9 us
  Pallas kernels  49.5 us (97%)
  local copies, waits for them, and re-layouts  0.66 us (1%)
  loops' own time  0.64 us (1%)
    pallas_call x1, Pallas kernels, one_pass(): pl.pallas_call(kernel, out_shape=(jax.ShapeDtypeStruct((ROWS, LANES), jnp...  49.5 us

profile of v3, /device:TPU:1, one launch (start us, length us, event | category | flops | bytes accessed | tf_op | source)
XLA Modules:
  0.0 50.9 jit_solution(1509196067398893590)
XLA Ops:
  0.0 0.0 copy-start.2
  0.0 0.0 copy-start.5
  0.0 0.0 copy-start.4
  0.0 0.0 copy-start.1
  0.0 0.0 copy-start.8
  0.0 0.0 copy-start.7
  0.0 0.0 copy-start.6
  0.0 0.0 copy-start.3
  0.1 0.0 copy-start
  0.1 49.5 %ladder.2 = (f32[96,128]{1,0:T(8,128)S(1)}, s32[1]{0:T(128)}) custom-call(s32[2,6]{1,0:T(2,128)} %bitcast.16, s32[128]{0:T(128)} %occ_irrep_in.1, s32[128]{0:T(128)} %slab_in.1, f32[128]{0:T(128)} %occ_energy_in.1, bf16[96,128,128]{2,1,0:T(8,128)(2,1)} %bitcast.9, bf16[2,128,128]{2,1,0:T(8,128)(2,1)} %ints_in.1, s32[1,128]{1,0:T(1,128)} %bitcast.18, ...), custom_call_target="tpu_custom_call" | custom-call | flops 100663296 | bytes 3145728 | tf_op jit(solution)/shard_map/ladder/pallas_call | solution.py:270
  49.6 0.0 copy-done.2
  49.6 0.0 copy-done.5
  49.6 0.0 copy-done.4
  49.6 0.0 copy-done.1
  49.6 0.0 copy-done.8
  49.6 0.0 copy-done.7
  49.6 0.0 copy-done.6
  49.7 0.0 copy-done.3
  49.7 0.0 copy-done
  49.7 0.6 %while.10 = (s32[]{:T(128)}, f32[96,128]{1,0:T(8,128)S(1)}, s32[1]{0:T(128)}, s32[2,6]{1,0:T(2,128)S(1)}, s32[128]{0:T(128)S(1)}, /*index=5*/s32[128]{0:T(128)S(...) while((s32[]{:T(128)}, f32[96,128]{1,0:T(8,128)S(1)}, ...), condition=%wide.region_1.0_spmd, body=%wide.region_0.0_spmd.sunk | while | flops 100675584 | bytes 3293853 | solution.py:330
  50.3 0.6 %copy.17 = f32[6,16,128]{2,1,0:T(8,128)} copy(f32[6,16,128]{2,1,0:T(8,128)S(1)} %bitcast.11) | data formatting | bytes 98304
Async XLA Ops:
  0.0 49.6 %copy-start.2 = (s32[128]{0:T(128)S(1)}, s32[128]{0:T(128)}, u32[]{:S(2)}) copy-start(s32[128]{0:T(128)} %slab_in.1) | copy-start | bytes 1540
  0.0 49.6 %copy-start.5 = (f32[128]{0:T(128)S(1)}, f32[128]{0:T(128)}, u32[]{:S(2)}) copy-start(f32[128]{0:T(128)} %occ_energy_in.1) | copy-start | bytes 1540
  0.0 49.6 %copy-start.4 = (s32[128]{0:T(128)S(1)}, s32[128]{0:T(128)}, u32[]{:S(2)}) copy-start(s32[128]{0:T(128)} %occ_irrep_in.1) | copy-start | bytes 1540
  0.0 49.6 %copy-start.1 = (bf16[2,128,128]{2,1,0:T(8,128)(2,1)S(1)}, bf16[2,128,128]{2,1,0:T(8,128)(2,1)}, u32[]{:S(2)}) copy-start(bf16[2,128,128]{2,1,0:T(8,128)(2,1)} %ints_in.1) | copy-start | bytes 196612
  0.0 49.6 %copy-start.8 = (f32[128]{0:T(128)S(1)}, f32[128]{0:T(128)}, u32[]{:S(2)}) copy-start(f32[128]{0:T(128)} %param.19) | copy-start | bytes 1540
  0.0 49.6 %copy-start.7 = (s32[128]{0:T(128)S(1)}, s32[128]{0:T(128)}, u32[]{:S(2)}) copy-start(s32[128]{0:T(128)} %param.17) | copy-start | bytes 1540
  0.0 49.6 %copy-start.6 = (s32[128]{0:T(128)S(1)}, s32[128]{0:T(128)}, u32[]{:S(2)}) copy-start(s32[128]{0:T(128)} %param.16) | copy-start | bytes 1540
  0.0 49.6 %copy-start.3 = (s32[6,2]{0,1:T(2,128)S(1)}, s32[6,2]{0,1:T(2,128)}, u32[]{:S(2)}) copy-start(s32[6,2]{0,1:T(2,128)} %param.13) | copy-start | bytes 148
  0.1 49.6 %copy-start = (bf16[6,16,128,128]{3,2,1,0:T(8,128)(2,1)S(1)}, bf16[6,16,128,128]{3,2,1,0:T(8,128)(2,1)}, u32[]{:S(2)}) copy-start(bf16[6,16,128,128]{3,2,1,0:T(8,128)(2,1)} %param.11) | copy-start | bytes 9437188

commit v4 on v3

--- a/solution.py
+++ b/solution.py
@@ -166,17 +166,19 @@
             pl.semaphore_wait(above.at[k], 1)
             copy.start()
 
-    for copy in near_z.values():
-        copy.wait_recv()
+    for k in (3, 2):
+        near_z[k].wait_recv()
     far_lo = {
-        k: push(blocks.at[core, 0, pl.ds(1, NZ - 1), 0], blocks.at[core, k, pl.ds(1, NZ - 1), 0], at(dy=k))
+        k: push(blocks.at[core, 0, pl.ds(2, NZ - 2), 0], blocks.at[core, k, pl.ds(2, NZ - 2), 0], at(dy=k))
         for k in FAR_FIRST
     }
+    near_z[1].wait_recv()
+    far_one = {k: push(blocks.at[core, 0, 1], blocks.at[core, k, 1], at(dy=k)) for k in FAR_FIRST}
     for copy in near_y:
         copy.wait_recv()
     far_hi = {
         k: push(blocks.at[core, pl.ds(1, NY - 1), 0, 1], blocks.at[core, pl.ds(1, NY - 1), k, 1], at(dz=k))
-        for k in range(1, NZ)
+        for k in range(2, NZ)
     }
 
     def share(part):
@@ -202,20 +204,28 @@
     for copy in shared:
         copy.wait_recv()
     total = contract_near(total, 1 - core)
-    shared_hi, shared_lo = [], []
+    shared_hi, shared_lo, shared_one = [], [], []
     for k, copy in far_hi.items():
         copy.wait_recv()
         shared_hi.append(share(blocks.at[core, pl.ds(1, NY - 1), k, 1]))
     for k in NEAR_FIRST:
         far_lo[k].wait_recv()
-        shared_lo.append(share(blocks.at[core, k, pl.ds(1, NZ - 1), 0]))
+        shared_lo.append(share(blocks.at[core, k, pl.ds(2, NZ - 2), 0]))
     for k in NEAR_FIRST:
-        total = contract(total, core, k, range(1, NZ))
+        total = contract(total, core, k, range(2, NZ))
+    for k in NEAR_FIRST:
+        far_one[k].wait_recv()
+        shared_one.append(share(blocks.at[core, k, 1]))
     for copy in shared_hi:
         copy.wait_recv()
     for k, copy in zip(NEAR_FIRST, shared_lo):
         copy.wait_recv()
-        total = contract(total, 1 - core, k, range(1, NZ))
+        total = contract(total, 1 - core, k, range(2, NZ))
+    for k in NEAR_FIRST:
+        total = contract(total, core, k, range(1, 2))
+    for k, copy in zip(NEAR_FIRST, shared_one):
+        copy.wait_recv()
+        total = contract(total, 1 - core, k, range(1, 2))
 
     @pl.when(half == 0)
     def _():
@@ -261,7 +271,7 @@
         copy.wait_send()
 
 
-N_COPIES = 10 + 10 + 12 + 7 + 3
+N_COPIES = 10 + 16 + 18 + 7 + 3
 
 
 def one_pass(collective_id, arrays):

time: 51.1 us -> 50.2 us (0.982)
  Pallas kernels: 49.5 us -> 48.7 us
    pallas_call x1, Pallas kernels: 49.5 us -> 48.7 us  [one_pass(): pl.pallas_call(kernel, out_shape=(jax.ShapeDtypeStruct((ROWS, LANES), jnp...]
where the time goes in v4:
time: 50.2 us; the launch traced here: 50.1 us
  Pallas kernels  48.7 us (97%)
  local copies, waits for them, and re-layouts  0.66 us (1%)
  loops' own time  0.64 us (1%)
    pallas_call x1, Pallas kernels, one_pass(): pl.pallas_call(kernel, out_shape=(jax.ShapeDtypeStruct((ROWS, LANES), jnp...  48.7 us

profile of v4, /device:TPU:1, one launch (start us, length us, event | category | flops | bytes accessed | tf_op | source)
XLA Modules:
  0.0 50.1 jit_solution(11387649495165587808)
XLA Ops:
  0.0 0.0 copy-start.2
  0.0 0.0 copy-start.5
  0.0 0.0 copy-start.4
  0.0 0.0 copy-start.1
  0.0 0.0 copy-start.8
  0.0 0.0 copy-start.7
  0.0 0.0 copy-start.6
  0.0 0.0 copy-start.3
  0.1 0.0 copy-start
  0.1 48.7 %ladder.2 = (f32[96,128]{1,0:T(8,128)S(1)}, s32[1]{0:T(128)}) custom-call(s32[2,6]{1,0:T(2,128)} %bitcast.16, s32[128]{0:T(128)} %occ_irrep_in.1, s32[128]{0:T(128)} %slab_in.1, f32[128]{0:T(128)} %occ_energy_in.1, bf16[96,128,128]{2,1,0:T(8,128)(2,1)} %bitcast.9, bf16[2,128,128]{2,1,0:T(8,128)(2,1)} %ints_in.1, s32[1,128]{1,0:T(1,128)} %bitcast.18, ...), custom_call_target="tpu_custom_call" | custom-call | flops 100663296 | bytes 3145728 | tf_op jit(solution)/shard_map/ladder/pallas_call | solution.py:280
  48.8 0.0 copy-done.2
  48.8 0.0 copy-done.5
  48.8 0.0 copy-done.4
  48.8 0.0 copy-done.1
  48.8 0.0 copy-done.8
  48.8 0.0 copy-done.7
  48.8 0.0 copy-done.6
  48.8 0.0 copy-done.3
  48.8 0.0 copy-done
  48.9 0.6 %while.10 = (s32[]{:T(128)}, f32[96,128]{1,0:T(8,128)S(1)}, s32[1]{0:T(128)}, s32[2,6]{1,0:T(2,128)S(1)}, s32[128]{0:T(128)S(1)}, /*index=5*/s32[128]{0:T(128)S(...) while((s32[]{:T(128)}, f32[96,128]{1,0:T(8,128)S(1)}, ...), condition=%wide.region_1.0_spmd, body=%wide.region_0.0_spmd.sunk | while | flops 100675584 | bytes 3293853 | solution.py:340
  49.5 0.6 %copy.17 = f32[6,16,128]{2,1,0:T(8,128)} copy(f32[6,16,128]{2,1,0:T(8,128)S(1)} %bitcast.11) | data formatting | bytes 98304
Async XLA Ops:
  0.0 48.8 %copy-start.2 = (s32[128]{0:T(128)S(1)}, s32[128]{0:T(128)}, u32[]{:S(2)}) copy-start(s32[128]{0:T(128)} %slab_in.1) | copy-start | bytes 1540
  0.0 48.8 %copy-start.5 = (f32[128]{0:T(128)S(1)}, f32[128]{0:T(128)}, u32[]{:S(2)}) copy-start(f32[128]{0:T(128)} %occ_energy_in.1) | copy-start | bytes 1540
  0.0 48.8 %copy-start.4 = (s32[128]{0:T(128)S(1)}, s32[128]{0:T(128)}, u32[]{:S(2)}) copy-start(s32[128]{0:T(128)} %occ_irrep_in.1) | copy-start | bytes 1540
  0.0 48.8 %copy-start.1 = (bf16[2,128,128]{2,1,0:T(8,128)(2,1)S(1)}, bf16[2,128,128]{2,1,0:T(8,128)(2,1)}, u32[]{:S(2)}) copy-start(bf16[2,128,128]{2,1,0:T(8,128)(2,1)} %ints_in.1) | copy-start | bytes 196612
  0.0 48.8 %copy-start.8 = (f32[128]{0:T(128)S(1)}, f32[128]{0:T(128)}, u32[]{:S(2)}) copy-start(f32[128]{0:T(128)} %param.19) | copy-start | bytes 1540
  0.0 48.8 %copy-start.7 = (s32[128]{0:T(128)S(1)}, s32[128]{0:T(128)}, u32[]{:S(2)}) copy-start(s32[128]{0:T(128)} %param.17) | copy-start | bytes 1540
  0.0 48.8 %copy-start.6 = (s32[128]{0:T(128)S(1)}, s32[128]{0:T(128)}, u32[]{:S(2)}) copy-start(s32[128]{0:T(128)} %param.16) | copy-start | bytes 1540
  0.0 48.8 %copy-start.3 = (s32[6,2]{0,1:T(2,128)S(1)}, s32[6,2]{0,1:T(2,128)}, u32[]{:S(2)}) copy-start(s32[6,2]{0,1:T(2,128)} %param.13) | copy-start | bytes 148
  0.1 48.8 %copy-start = (bf16[6,16,128,128]{3,2,1,0:T(8,128)(2,1)S(1)}, bf16[6,16,128,128]{3,2,1,0:T(8,128)(2,1)}, u32[]{:S(2)}) copy-start(bf16[6,16,128,128]{3,2,1,0:T(8,128)(2,1)} %param.11) | copy-start | bytes 9437188
